TPU v7x, 32 devices: a whole 2x2x4 slice. The times are simulated.
32 devices in a mesh: dp: 16 (over z, y, x), fsdp: 2 (over core).
Axes of the slice: x: 2, y: 2, z: 4, core: 2. Of those that a mesh axis runs over, the one named last changes fastest.
Arguments:
- tokens: bfloat16 [64, 196, 512], P(('dp', 'fsdp')), may hold values from -6 to 6
- regions: int32 [196], replicated, may hold values from 0 to 3
- rel_index: int32 [2401], replicated, may hold values from 0 to 168
- norm_gains: bfloat16 [2, 2, 512], P(None, None, 'fsdp'), may hold values from 0.5 to 1.5
- norm_shifts: bfloat16 [2, 2, 512], P(None, None, 'fsdp'), may hold values from -1.75 to 1.75
- qkv_weight: bfloat16 [2, 512, 1536], P(None, 'fsdp'), may hold values from -0.25 to 0.25
- qv_bias: bfloat16 [2, 2, 512], P(None, None, 'fsdp'), may hold values from -1.75 to 1.75
- rel_table: bfloat16 [2, 169, 16], P(None, None, 'fsdp'), may hold values from -6 to 6
- proj_weight: bfloat16 [2, 512, 512], P(None, 'fsdp'), may hold values from -0.75 to 0.75
- proj_bias: bfloat16 [2, 512], P(None, 'fsdp'), may hold values from -1.75 to 1.75
- fc1_weight: bfloat16 [2, 512, 2048], P(None, 'fsdp'), may hold values from -0.25 to 0.25
- fc1_bias: bfloat16 [2, 2048], P(None, 'fsdp'), may hold values from -1.75 to 1.75
- fc2_weight: bfloat16 [2, 2048, 512], P(None, 'fsdp'), may hold values from -0.1875 to 0.1875
- fc2_bias: bfloat16 [2, 512], P(None, 'fsdp'), may hold values from -1.75 to 1.75
- cotangent: bfloat16 [64, 196, 512], P(('dp', 'fsdp')), may hold values from -6 to 6
Outputs:
- output: bfloat16 [64, 196, 512], P(('dp', 'fsdp'))
- tokens_grad: float32 [64, 196, 512], P(('dp', 'fsdp'))
- norm_gains_grad: float32 [2, 2, 512], P(None, None, 'fsdp')
- norm_shifts_grad: float32 [2, 2, 512], P(None, None, 'fsdp')
- qkv_weight_grad: float32 [2, 512, 1536], P(None, 'fsdp')
- qv_bias_grad: float32 [2, 2, 512], P(None, None, 'fsdp')
- rel_table_grad: float32 [2, 169, 16], P(None, None, 'fsdp')
- proj_weight_grad: float32 [2, 512, 512], P(None, 'fsdp')
- proj_bias_grad: float32 [2, 512], P(None, 'fsdp')
- fc1_weight_grad: float32 [2, 512, 2048], P(None, 'fsdp')
- fc1_bias_grad: float32 [2, 2048], P(None, 'fsdp')
- fc2_weight_grad: float32 [2, 2048, 512], P(None, 'fsdp')
- fc2_bias_grad: float32 [2, 512], P(None, 'fsdp')
All inputs are finite; a program needn't handle non-finite values.
Results may differ from a plain program's by a relative error of at most 0.018.
Values may be sent and summed in bfloat16 or wider, within the bound.
No kernel may reach another device: no remote copies, remote signals or barrier semaphores. Data moves between devices by JAX's collectives and lax.ppermute only.
A program may use at most 192 MiB of HBM per device.

v0:
```python
import jax
import jax.numpy as jnp
from jax import lax
from jax.sharding import PartitionSpec as P

D = 512
HEADS = 16
HD = 32
WIN = 7
IMG = 14
SHIFT = 3
MICRO = 2
PIX = 196
WT = 49
RELS = 169


norm_eps = 1e-05
highest = lax.Precision.HIGHEST


def layer_norm(values, gain_in, shift_in):
    average = jnp.mean(values, -1, keepdims=True)
    centred = values - average
    variance = jnp.mean(centred * centred, -1, keepdims=True)
    return centred * lax.rsqrt(variance + norm_eps) * gain_in + shift_in


def to_windows(values, offset):
    images = values.shape[0]
    channels = values.shape[-1]
    across = IMG // WIN
    canvas = values.reshape(images, IMG, IMG, channels)
    if offset:
        canvas = jnp.roll(canvas, (-offset, -offset), axis=(1, 2))
    canvas = canvas.reshape(images, across, WIN, across, WIN, channels).transpose(0, 1, 3, 2, 4, 5)
    return canvas.reshape(images * across * across, WIN * WIN, channels)


def from_windows(windows, images, offset):
    channels = windows.shape[-1]
    across = IMG // WIN
    canvas = windows.reshape(images, across, across, WIN, WIN, channels).transpose(0, 1, 3, 2, 4, 5)
    canvas = canvas.reshape(images, IMG, IMG, channels)
    if offset:
        canvas = jnp.roll(canvas, (offset, offset), axis=(1, 2))
    return canvas.reshape(images, IMG * IMG, channels)


def split_heads(rows_in):
    return rows_in.reshape(-1, WT, HEADS, HD)


def attend_probs(queries, keys_all, table, region_mask, onehot_low):
    bias_rows = jnp.dot(onehot_low, table, preferred_element_type=jnp.float32)
    position_bias = bias_rows.T.reshape(HEADS, WT, WT)
    scores = (
        HD ** (-0.5)
        * jnp.einsum("wqhc,wkhc->whqk", queries, keys_all, preferred_element_type=jnp.float32)
        + position_bias[None]
    )
    if region_mask is not None:
        scores = scores + region_mask[:, None]
    largest = jnp.max(scores, -1, keepdims=True)
    expo = jnp.exp(scores - largest)
    return expo / jnp.sum(expo, -1, keepdims=True)


def exact_gelu(inner):
    return jax.nn.gelu(inner, approximate=False)


def layer_forward(tokens_in, params, offset, region_mask, onehot_low):
    gains, shifts_in, qkv_w, qv_b, table, proj_w, proj_b, up_w, up_b, down_w, down_b = params
    images = tokens_in.shape[0]
    gain_f = gains.astype(jnp.float32)
    shift_f = shifts_in.astype(jnp.float32)
    normed = layer_norm(tokens_in, gain_f[0], shift_f[0]).astype(jnp.bfloat16)
    windows = to_windows(normed, offset).reshape(-1, D)
    projected = jnp.dot(windows, qkv_w, preferred_element_type=jnp.float32)
    bias_f = qv_b.astype(jnp.float32)
    queries = split_heads((projected[:, :D] + bias_f[0]).astype(jnp.bfloat16))
    keys_all = split_heads(projected[:, D : 2 * D].astype(jnp.bfloat16))
    values_all = split_heads((projected[:, 2 * D :] + bias_f[1]).astype(jnp.bfloat16))
    probs = attend_probs(queries, keys_all, table, region_mask, onehot_low)
    attended = jnp.einsum(
        "whqk,wkhc->wqhc",
        probs.astype(jnp.bfloat16),
        values_all,
        preferred_element_type=jnp.float32,
    )
    attended = attended.astype(jnp.bfloat16).reshape(-1, D)
    branch = jnp.dot(attended, proj_w, preferred_element_type=jnp.float32) + proj_b.astype(
        jnp.float32
    )
    middle = tokens_in + from_windows(branch.reshape(-1, WT, D), images, offset)
    normed_two = layer_norm(middle, gain_f[1], shift_f[1]).astype(jnp.bfloat16).reshape(-1, D)
    hidden_pre = jnp.dot(normed_two, up_w, preferred_element_type=jnp.float32) + up_b.astype(
        jnp.float32
    )
    hidden = exact_gelu(hidden_pre).astype(jnp.bfloat16)
    mlp_out = jnp.dot(hidden, down_w, preferred_element_type=jnp.float32) + down_b.astype(
        jnp.float32
    )
    result = middle + mlp_out.reshape(middle.shape)
    return (
        result,
        (
            tokens_in,
            windows,
            queries,
            keys_all,
            values_all,
            attended,
            middle,
            normed_two,
            hidden_pre,
            hidden,
        ),
    )


def layer_backward(grad_out, saved, params, offset, region_mask, onehot_low, onehot_full):
    gains, shifts_in, qkv_w, qv_b, table, proj_w, proj_b, up_w, up_b, down_w, down_b = params
    (
        tokens_in,
        windows,
        queries,
        keys_all,
        values_all,
        attended,
        middle,
        normed_two,
        hidden_pre,
        hidden,
    ) = saved
    images = tokens_in.shape[0]
    gain_f = gains.astype(jnp.float32)
    shift_f = shifts_in.astype(jnp.float32)
    mlp_grad = grad_out.reshape(-1, D).astype(jnp.bfloat16)
    down_b_grad = jnp.sum(mlp_grad.astype(jnp.float32), 0)
    hidden_grad = jnp.einsum("nd,fd->nf", mlp_grad, down_w, preferred_element_type=jnp.float32)
    gelu_out, gelu_pull = jax.vjp(exact_gelu, hidden_pre)
    pre_grad = gelu_pull(hidden_grad)[0].astype(jnp.bfloat16)
    up_b_grad = jnp.sum(pre_grad.astype(jnp.float32), 0)
    normed_two_grad = jnp.einsum("nf,df->nd", pre_grad, up_w, preferred_element_type=jnp.float32)
    norm_out, norm_pull = jax.vjp(layer_norm, middle, gain_f[1], shift_f[1])
    middle_part, gain_two_grad, shift_two_grad = norm_pull(normed_two_grad.reshape(middle.shape))
    middle_grad = grad_out + middle_part
    branch_grad = to_windows(middle_grad, offset).reshape(-1, D).astype(jnp.bfloat16)
    proj_b_grad = jnp.sum(branch_grad.astype(jnp.float32), 0)
    attended_grad = jnp.einsum("ne,de->nd", branch_grad, proj_w, preferred_element_type=jnp.float32)
    attended_grad = split_heads(attended_grad.astype(jnp.bfloat16))
    probs = attend_probs(queries, keys_all, table, region_mask, onehot_low)
    probs_grad = jnp.einsum(
        "wqhc,wkhc->whqk", attended_grad, values_all, preferred_element_type=jnp.float32
    )
    values_grad = jnp.einsum(
        "whqk,wqhc->wkhc",
        probs.astype(jnp.bfloat16),
        attended_grad,
        preferred_element_type=jnp.float32,
    ).astype(jnp.bfloat16)
    row_delta = jnp.sum(probs_grad * probs, -1, keepdims=True)
    scores_grad = (probs * (probs_grad - row_delta)).astype(jnp.bfloat16)
    head_scale = HD ** (-0.5)
    queries_grad = (
        head_scale
        * jnp.einsum("whqk,wkhc->wqhc", scores_grad, keys_all, preferred_element_type=jnp.float32)
    ).astype(jnp.bfloat16)
    keys_grad = (
        head_scale
        * jnp.einsum("whqk,wqhc->wkhc", scores_grad, queries, preferred_element_type=jnp.float32)
    ).astype(jnp.bfloat16)
    pair_grad = jnp.sum(scores_grad.astype(jnp.float32), 0).reshape(HEADS, WT * WT)
    table_grad = jnp.dot(pair_grad, onehot_full, precision=highest).T
    queries_flat = queries_grad.reshape(-1, D)
    values_flat = values_grad.reshape(-1, D)
    joined_grad = jnp.concatenate([queries_flat, keys_grad.reshape(-1, D), values_flat], axis=1)
    qv_b_grad = jnp.stack(
        [jnp.sum(queries_flat.astype(jnp.float32), 0), jnp.sum(values_flat.astype(jnp.float32), 0)]
    )
    normed_grad = jnp.einsum("ne,de->nd", joined_grad, qkv_w, preferred_element_type=jnp.float32)
    normed_grad = from_windows(normed_grad.reshape(-1, WT, D), images, offset)
    first_out, first_pull = jax.vjp(layer_norm, tokens_in, gain_f[0], shift_f[0])
    input_part, gain_one_grad, shift_one_grad = first_pull(normed_grad)
    input_grad = middle_grad + input_part
    small = [
        jnp.stack([gain_one_grad, gain_two_grad]),
        jnp.stack([shift_one_grad, shift_two_grad]),
        qv_b_grad,
        table_grad,
        proj_b_grad,
        up_b_grad,
        down_b_grad,
    ]
    factors = [
        (windows, joined_grad),
        (attended, branch_grad),
        (normed_two, pre_grad),
        (hidden, mlp_grad),
    ]
    return (input_grad, small, factors)


def fetch_forward(shards, layer_at):
    return (
        lax.all_gather(shards[0][layer_at], "fsdp", axis=1, tiled=True),
        lax.all_gather(shards[1][layer_at], "fsdp", axis=1, tiled=True),
        lax.all_gather(shards[2][layer_at], "fsdp", axis=0, tiled=True),
        lax.all_gather(shards[3][layer_at], "fsdp", axis=1, tiled=True),
        lax.all_gather(shards[4][layer_at], "fsdp", axis=1, tiled=True),
        lax.all_gather(shards[5][layer_at], "fsdp", axis=0, tiled=True),
        lax.all_gather(shards[6][layer_at], "fsdp", axis=0, tiled=True),
        lax.all_gather(shards[7][layer_at], "fsdp", axis=0, tiled=True),
        lax.all_gather(shards[8][layer_at], "fsdp", axis=0, tiled=True),
        lax.all_gather(shards[9][layer_at], "fsdp", axis=0, tiled=True),
        lax.all_gather(shards[10][layer_at], "fsdp", axis=0, tiled=True),
    )


def fetch_backward(shards, layer_at):
    return (
        lax.all_gather(shards[0][layer_at], "fsdp", axis=1, tiled=True),
        lax.all_gather(shards[1][layer_at], "fsdp", axis=1, tiled=True),
        lax.all_gather(shards[2][layer_at], "fsdp", axis=0, tiled=True),
        lax.all_gather(shards[3][layer_at], "fsdp", axis=1, tiled=True),
        lax.all_gather(shards[4][layer_at], "fsdp", axis=1, tiled=True),
        lax.all_gather(shards[5][layer_at], "fsdp", axis=0, tiled=True),
        lax.all_gather(shards[6][layer_at], "fsdp", axis=0, tiled=True),
        lax.all_gather(shards[7][layer_at], "fsdp", axis=0, tiled=True),
        lax.all_gather(shards[8][layer_at], "fsdp", axis=0, tiled=True),
        lax.all_gather(shards[9][layer_at], "fsdp", axis=0, tiled=True),
        lax.all_gather(shards[10][layer_at], "fsdp", axis=0, tiled=True),
    )


def body(
    tokens,
    regions,
    rel_index,
    norm_gains,
    norm_shifts,
    qkv_weight,
    qv_bias,
    rel_table,
    proj_weight,
    proj_bias,
    fc1_weight,
    fc1_bias,
    fc2_weight,
    fc2_bias,
    cotangent,
):
    shards = (
        norm_gains,
        norm_shifts,
        qkv_weight,
        qv_bias,
        rel_table,
        proj_weight,
        proj_bias,
        fc1_weight,
        fc1_bias,
        fc2_weight,
        fc2_bias,
    )
    offsets_all = jnp.arange(RELS, dtype=jnp.int32)
    onehot_full = (rel_index[:, None] == offsets_all[None, :]).astype(jnp.float32)
    onehot_low = onehot_full.astype(jnp.bfloat16)
    region_win = to_windows(regions.reshape(1, PIX, 1), 0).reshape(-1, WT)
    region_base = jnp.where(region_win[:, :, None] == region_win[:, None, :], 0.0, -100.0).astype(
        jnp.float32
    )
    per_batch = tokens.shape[0] // MICRO
    region_mask = jnp.tile(region_base, (per_batch, 1, 1))
    small_totals = [None, None]
    factor_lists = [[], []]
    outputs = []
    input_grads = []
    for batch_at in range(MICRO):
        current = tokens[batch_at * per_batch : (batch_at + 1) * per_batch].astype(jnp.float32)
        grad_now = cotangent[batch_at * per_batch : (batch_at + 1) * per_batch].astype(jnp.float32)
        gathered_all = []
        saved_all = []
        for layer_at in range(2):
            gathered = fetch_forward(shards, layer_at)
            current, saved = layer_forward(
                current, gathered, layer_at * SHIFT, region_mask if layer_at else None, onehot_low
            )
            gathered_all.append(gathered)
            saved_all.append(saved)
        outputs.append(current.astype(jnp.bfloat16))
        for layer_at in (1, 0):
            params = fetch_backward(shards, layer_at)
            grad_now, small, factors = layer_backward(
                grad_now,
                saved_all[layer_at],
                params,
                layer_at * SHIFT,
                region_mask if layer_at else None,
                onehot_low,
                onehot_full,
            )
            factor_lists[layer_at].append(factors)
            if small_totals[layer_at] is None:
                small_totals[layer_at] = small
            else:
                small_totals[layer_at] = [
                    older + newer for older, newer in zip(small_totals[layer_at], small)
                ]
        input_grads.append(grad_now)
    full_grads = []
    for layer_at in range(2):
        matrices = []
        for factor_at in range(4):
            left = jnp.concatenate(
                [entry[factor_at][0] for entry in factor_lists[layer_at]], axis=0
            )
            right = jnp.concatenate(
                [entry[factor_at][1] for entry in factor_lists[layer_at]], axis=0
            )
            matrices.append(
                jnp.einsum("na,nb->ab", left, right, preferred_element_type=jnp.float32)
            )
        small = small_totals[layer_at]
        full_grads.append(
            [
                small[0],
                small[1],
                matrices[0],
                small[2],
                small[3],
                matrices[1],
                small[4],
                matrices[2],
                small[5],
                matrices[3],
                small[6],
            ]
        )
    stacked = tuple(
        (jnp.stack([full_grads[0][param_at], full_grads[1][param_at]]) for param_at in range(11))
    )
    owned = (
        lax.psum_scatter(
            stacked[0].astype(jnp.bfloat16), "fsdp", scatter_dimension=2, tiled=True
        ).astype(jnp.float32),
        lax.psum_scatter(
            stacked[1].astype(jnp.bfloat16), "fsdp", scatter_dimension=2, tiled=True
        ).astype(jnp.float32),
        lax.psum_scatter(
            stacked[2].astype(jnp.bfloat16), "fsdp", scatter_dimension=1, tiled=True
        ).astype(jnp.float32),
        lax.psum_scatter(
            stacked[3].astype(jnp.bfloat16), "fsdp", scatter_dimension=2, tiled=True
        ).astype(jnp.float32),
        lax.psum_scatter(
            stacked[4].astype(jnp.bfloat16), "fsdp", scatter_dimension=2, tiled=True
        ).astype(jnp.float32),
        lax.psum_scatter(
            stacked[5].astype(jnp.bfloat16), "fsdp", scatter_dimension=1, tiled=True
        ).astype(jnp.float32),
        lax.psum_scatter(
            stacked[6].astype(jnp.bfloat16), "fsdp", scatter_dimension=1, tiled=True
        ).astype(jnp.float32),
        lax.psum_scatter(
            stacked[7].astype(jnp.bfloat16), "fsdp", scatter_dimension=1, tiled=True
        ).astype(jnp.float32),
        lax.psum_scatter(
            stacked[8].astype(jnp.bfloat16), "fsdp", scatter_dimension=1, tiled=True
        ).astype(jnp.float32),
        lax.psum_scatter(
            stacked[9].astype(jnp.bfloat16), "fsdp", scatter_dimension=1, tiled=True
        ).astype(jnp.float32),
        lax.psum_scatter(
            stacked[10].astype(jnp.bfloat16), "fsdp", scatter_dimension=1, tiled=True
        ).astype(jnp.float32),
    )
    results = lax.psum(
        (
            owned[0],
            owned[1],
            owned[2],
            owned[3],
            owned[4],
            owned[5],
            owned[6],
            owned[7],
            owned[8],
            owned[9],
            owned[10],
        ),
        "dp",
    )
    output = jnp.concatenate(outputs, axis=0)
    tokens_grad = jnp.concatenate(input_grads, axis=0)
    return (
        output,
        tokens_grad,
        results[0],
        results[1],
        results[2],
        results[3],
        results[4],
        results[5],
        results[6],
        results[7],
        results[8],
        results[9],
        results[10],
    )


def solution(mesh):
    return jax.shard_map(
        body,
        mesh=mesh,
        in_specs=(
            P(("dp", "fsdp"), None, None),
            P(),
            P(),
            P(None, None, "fsdp"),
            P(None, None, "fsdp"),
            P(None, "fsdp", None),
            P(None, None, "fsdp"),
            P(None, None, "fsdp"),
            P(None, "fsdp", None),
            P(None, "fsdp"),
            P(None, "fsdp", None),
            P(None, "fsdp"),
            P(None, "fsdp", None),
            P(None, "fsdp"),
            P(("dp", "fsdp"), None, None),
        ),
        out_specs=(
            P(("dp", "fsdp"), None, None),
            P(("dp", "fsdp"), None, None),
            P(None, None, "fsdp"),
            P(None, None, "fsdp"),
            P(None, "fsdp", None),
            P(None, None, "fsdp"),
            P(None, None, "fsdp"),
            P(None, "fsdp", None),
            P(None, "fsdp"),
            P(None, "fsdp", None),
            P(None, "fsdp"),
            P(None, "fsdp", None),
            P(None, "fsdp"),
        ),
        check_vma=False,
    )
```

profile of v0, /device:TPU:0, one launch (start us, length us, event | category | flops | bytes accessed | tf_op | source)
XLA Modules:
  0.0 1043.0 jit_solution(15488071941158897186)
XLA Ops:
  9.9 3.1 fusion.347
  13.1 3.1 fusion.346
  73.3 3.7 fusion.365
  88.3 2.6 copy.215
  92.3 2.6 copy.217
  94.9 3.3 fusion.366
  104.4 7.3 multiply_convert_fusion.5
  111.7 2.7 fusion.368
  114.7 5.2 multiply_convert_fusion.7
  144.0 4.2 fusion.369
  176.8 4.6 fusion.370
  196.1 7.6 multiply_convert_fusion.6
  203.6 5.3 multiply_convert_fusion.4
  209.0 4.5 convert_reduce_fusion.4
  241.4 3.0 convert_reduce_fusion.10
  292.8 3.0 convert_reduce_fusion.8
  345.7 4.5 multiply_reduce_fusion.2
  418.2 2.6 fusion.6
  447.5 3.5 all-reduce
  457.2 9.3 reduce-scatter.26.cloned.1.call-done
  466.5 14.8 %reduce-scatter.24.cloned.1.call-done = bf16[2,256,1536]{2,1,0:T(8,128)(2,1)} async-done(((bf16[2,512,1536]{2,1,0:T(8,128)(2,1)}), bf16[2,256,1536]{2,1,0:T(8,128)(2,1)}) %reduce-scatter.24.cloned.1.call-update) | async-done | bytes 1572880 | tf_op jit(solution)/shard_map/reduce_scatter | solution.py:352
  481.3 16.1 %reduce-scatter.30.cloned.1.call-done = bf16[2,1024,512]{2,1,0:T(8,128)(2,1)} async-done(((bf16[2,2048,512]{2,1,0:T(8,128)(2,1)}), bf16[2,1024,512]{2,1,0:T(8,128)(2,1)}) %reduce-scatter.30.cloned.1.call-update) | async-done | bytes 2097168 | tf_op jit(solution)/shard_map/reduce_scatter | solution.py:373
  497.3 16.1 %reduce-scatter.28.cloned.1.call-done = bf16[2,256,2048]{2,1,0:T(8,128)(2,1)} async-done(((bf16[2,512,2048]{2,1,0:T(8,128)(2,1)}), bf16[2,256,2048]{2,1,0:T(8,128)(2,1)}) %reduce-scatter.28.cloned.1.call-update) | async-done | bytes 2097168 | tf_op jit(solution)/shard_map/reduce_scatter | solution.py:367
  513.4 522.8 %all-reduce.3 = (f32[2,2,256]{2,1,0:T(2,128)}, f32[2,2,256]{2,1,0:T(2,128)}, f32[2,256,1536]{2,1,0:T(8,128)}, f32[2,2,256]{2,1,0:T(2,128)}, f32[2,169,8]{1,2,0:T...) all-reduce(bf16[2,2,256]{2,1,0:T(2,128)(2,1)S(1)} %copy.347, ...), channel_id=1, replica_groups=mesh['dp'=16,'fsdp'=2] {'dp'}, use_global_device_ids=true, to_apply=%region_53.54 | all-reduce | flops 3154576 | bytes 18932864 | tf_op jit(solution)/shard_map/psum | solution.py:380
  (936 shorter events, 368.8 us)
Async XLA Ops:
  7.2 53.4 %all-gather.29.cloned.1.call-start = ((), (), s32[]{:S(2)}) async-start(), calls=%async_computation.14 | async-start | bytes 2359296 | tf_op jit(solution)/shard_map/all_gather | solution.py:210
  9.9 94.5 %all-gather.31.cloned.1.call-start = ((), (), s32[]{:S(2)}) async-start(), calls=%async_computation.15 | async-start | bytes 3145728 | tf_op jit(solution)/shard_map/all_gather | solution.py:215
  13.0 98.7 %all-gather.33.cloned.1.call-start = ((), (), s32[]{:S(2)}) async-start(), calls=%async_computation.16 | async-start | bytes 3145728 | tf_op jit(solution)/shard_map/all_gather | solution.py:217
  16.3 107.7 %all-gather.35.cloned.1.call-start = ((), (), s32[]{:S(2)}) async-start(), calls=%async_computation.17 | async-start | bytes 2359296 | tf_op jit(solution)/shard_map/all_gather | solution.py:210
  16.8 179.2 %all-gather.37.cloned.1.call-start = ((), (), s32[]{:S(2)}) async-start(), calls=%async_computation.18 | async-start | bytes 3145728 | tf_op jit(solution)/shard_map/all_gather | solution.py:215
  17.4 191.5 %all-gather.39.cloned.1.call-start = ((), (), s32[]{:S(2)}) async-start(), calls=%async_computation.19 | async-start | bytes 3145728 | tf_op jit(solution)/shard_map/all_gather | solution.py:217
  18.0 433.0 %reduce-scatter.42.cloned.1.call-start = ((), (), s32[]{:S(2)}) async-start(), calls=%async_computation.25 | async-start | bytes 196608
  18.8 63.3 %copy-start.19 = (bf16[1,196,512]{2,1,0:T(8,128)(2,1)}, bf16[1,196,512]{2,1,0:T(8,128)(2,1)S(1)}, u32[]{:S(2)}) copy-start(bf16[1,196,512]{2,1,0:T(8,128)(2,1)S(1)} %get-tuple-element.145) | copy-start | bytes 602116
  19.2 84.5 %copy-start.17 = (bf16[1,196,512]{2,1,0:T(8,128)(2,1)}, bf16[1,196,512]{2,1,0:T(8,128)(2,1)S(1)}, u32[]{:S(2)}) copy-start(bf16[1,196,512]{2,1,0:T(8,128)(2,1)S(1)} %get-tuple-element.135) | copy-start | bytes 602116
  22.3 81.8 %copy-start.131 = (f32[1,1,512]{2,1,0:T(1,128)}, f32[1,1,512]{2,1,0:T(1,128)S(1)}, u32[]{:S(2)}) copy-start(f32[1,1,512]{2,1,0:T(1,128)S(1)} %get-tuple-element.207) | copy-start | bytes 6148
  24.6 35.9 %copy-start.72 = (bf16[196,512]{1,0:T(8,128)(2,1)}, bf16[196,512]{1,0:T(8,128)(2,1)S(1)}, u32[]{:S(2)}) copy-start(bf16[196,512]{1,0:T(8,128)(2,1)S(1)} %reshape_reshape.67) | copy-start | bytes 602116
  24.8 38.4 %copy-start.74 = (bf16[196,512]{1,0:T(8,128)(2,1)}, bf16[196,512]{1,0:T(8,128)(2,1)S(1)}, u32[]{:S(2)}) copy-start(bf16[196,512]{1,0:T(8,128)(2,1)S(1)} %reshape_reshape.61) | copy-start | bytes 602116
  32.6 69.3 %copy-start.2 = (bf16[1,512,512]{2,1,0:T(8,128)(2,1)}, bf16[1,512,512]{2,1,0:T(8,128)(2,1)S(1)}, u32[]{:S(2)}) copy-start(bf16[1,512,512]{2,1,0:T(8,128)(2,1)S(1)} %all-gather.5) | copy-start | bytes 1572868
  41.0 80.5 %copy-start.133 = (f32[1,1,512]{2,1,0:T(1,128)}, f32[1,1,512]{2,1,0:T(1,128)S(1)}, u32[]{:S(2)}) copy-start(f32[1,1,512]{2,1,0:T(1,128)S(1)} %get-tuple-element.196) | copy-start | bytes 6148
  82.2 29.5 %copy-start.7 = (f32[1,196,512]{2,1,0:T(8,128)}, f32[1,196,512]{2,1,0:T(8,128)S(1)}, u32[]{:S(2)}) copy-start(f32[1,196,512]{2,1,0:T(8,128)S(1)} %get-tuple-element.143) | copy-start | bytes 1204228
  370.1 81.9 %reduce-scatter.38.cloned.1.call-start = ((), (), s32[]{:S(2)}) async-start(), calls=%async_computation.23 | async-start | bytes 196608
  400.0 52.9 %reduce-scatter.36.cloned.1.call-start = ((), (), s32[]{:S(2)}) async-start(), calls=%async_computation.22 | async-start | bytes 196608
  401.3 52.7 %reduce-scatter.34.cloned.1.call-start = ((), (), s32[]{:S(2)}) async-start(), calls=%async_computation.21 | async-start | bytes 196608
  402.6 52.5 %reduce-scatter.32.cloned.1.call-start = ((), (), s32[]{:S(2)}) async-start(), calls=%async_computation.20 | async-start | bytes 196608
  406.6 49.5 %reduce-scatter.40.cloned.1.call-start = ((), (), s32[]{:S(2)}) async-start(), calls=%async_computation.24 | async-start | bytes 786432
  409.2 57.4 %reduce-scatter.26.cloned.1.call-start = ((), (), s32[]{:S(2)}) async-start(), calls=%async_computation.11 | async-start | bytes 1572864 | tf_op jit(solution)/shard_map/reduce_scatter | solution.py:361
  411.6 69.6 %reduce-scatter.24.cloned.1.call-start = ((), (), s32[]{:S(2)}) async-start(), calls=%async_computation.10 | async-start | bytes 4718592 | tf_op jit(solution)/shard_map/reduce_scatter | solution.py:352
  416.9 80.4 %reduce-scatter.30.cloned.1.call-start = ((), (), s32[]{:S(2)}) async-start(), calls=%async_computation.13 | async-start | bytes 6291456 | tf_op jit(solution)/shard_map/reduce_scatter | solution.py:373
  424.6 88.7 %reduce-scatter.28.cloned.1.call-start = ((), (), s32[]{:S(2)}) async-start(), calls=%async_computation.12 | async-start | bytes 6291456 | tf_op jit(solution)/shard_map/reduce_scatter | solution.py:367
  (237 other events, 735.2 us)
Sparse Core Ops, SparseCore 0:
  10.1 12.4 all-gather.28
  24.8 11.7 all-gather.30
  38.1 11.7 all-gather.32
  51.3 10.9 all-gather.34
  64.3 11.7 all-gather.36
  77.5 11.7 all-gather.38
  370.2 9.9 reduce-scatter.41
  400.1 9.9 reduce-scatter.37
  412.3 8.6 reduce-scatter.35
  423.0 8.6 reduce-scatter.33
  433.9 8.6 reduce-scatter.31
  444.7 9.1 reduce-scatter.39
  456.8 9.6 reduce-scatter.25
  469.2 12.0 reduce-scatter.23
  484.1 13.1 reduce-scatter.29
  500.0 13.2 reduce-scatter.27
where the time goes:
time: 1050 us; the launch traced here: 1040 us
  blocking collectives  557 us (53%)
  local copies, waits for them, and re-layouts  223 us (21%)
  matrix products  143 us (14%)
  waiting for transfers between devices  58.1 us (6%)
  other arithmetic  42.7 us (4%)
  between operations  18.7 us (2%)
    psum x1, blocking collectives, body(): lax.psum((owned[0], owned[1], owned[2], owned[3], owned[4], owned[5], own...  523 us
    reshape x32, local copies, waits for them, and re-layouts, split_heads(): return rows_in.reshape(-1, WT, HEADS, HD)  65.2 us
    unnamed x519, local copies, waits for them, and re-layouts  37.8 us
    dot_general x4, matrix products, layer_forward(): jnp.dot(normed_two, up_w, preferred_element_type=jnp.float32)  25.4 us
  transfers between devices with their start and end apart: 16, of which 4 were waited for; matrix products, arithmetic and copies ran while one was open for 23% of the time, Pallas kernels for 0%

commit v1 on v0

--- a/solution.py
+++ b/solution.py
@@ -9,7 +9,6 @@
 WIN = 7
 IMG = 14
 SHIFT = 3
-MICRO = 2
 PIX = 196
 WT = 49
 RELS = 169
@@ -203,36 +202,72 @@
     return (input_grad, small, factors)
 
 
-def fetch_forward(shards, layer_at):
-    return (
-        lax.all_gather(shards[0][layer_at], "fsdp", axis=1, tiled=True),
-        lax.all_gather(shards[1][layer_at], "fsdp", axis=1, tiled=True),
-        lax.all_gather(shards[2][layer_at], "fsdp", axis=0, tiled=True),
-        lax.all_gather(shards[3][layer_at], "fsdp", axis=1, tiled=True),
-        lax.all_gather(shards[4][layer_at], "fsdp", axis=1, tiled=True),
-        lax.all_gather(shards[5][layer_at], "fsdp", axis=0, tiled=True),
-        lax.all_gather(shards[6][layer_at], "fsdp", axis=0, tiled=True),
-        lax.all_gather(shards[7][layer_at], "fsdp", axis=0, tiled=True),
-        lax.all_gather(shards[8][layer_at], "fsdp", axis=0, tiled=True),
-        lax.all_gather(shards[9][layer_at], "fsdp", axis=0, tiled=True),
-        lax.all_gather(shards[10][layer_at], "fsdp", axis=0, tiled=True),
-    )
-
-
-def fetch_backward(shards, layer_at):
-    return (
-        lax.all_gather(shards[0][layer_at], "fsdp", axis=1, tiled=True),
-        lax.all_gather(shards[1][layer_at], "fsdp", axis=1, tiled=True),
-        lax.all_gather(shards[2][layer_at], "fsdp", axis=0, tiled=True),
-        lax.all_gather(shards[3][layer_at], "fsdp", axis=1, tiled=True),
-        lax.all_gather(shards[4][layer_at], "fsdp", axis=1, tiled=True),
-        lax.all_gather(shards[5][layer_at], "fsdp", axis=0, tiled=True),
-        lax.all_gather(shards[6][layer_at], "fsdp", axis=0, tiled=True),
-        lax.all_gather(shards[7][layer_at], "fsdp", axis=0, tiled=True),
-        lax.all_gather(shards[8][layer_at], "fsdp", axis=0, tiled=True),
-        lax.all_gather(shards[9][layer_at], "fsdp", axis=0, tiled=True),
-        lax.all_gather(shards[10][layer_at], "fsdp", axis=0, tiled=True),
-    )
+def swap_cores(value):
+    return lax.ppermute(value, "fsdp", [(0, 1), (1, 0)])
+
+
+def gather_cores(own, axis):
+    other = swap_cores(own)
+    first = lax.axis_index("fsdp") == 0
+    return jnp.concatenate([jnp.where(first, own, other), jnp.where(first, other, own)], axis=axis)
+
+
+def add_low(one, two):
+    return (one.astype(jnp.float32) + two.astype(jnp.float32)).astype(jnp.bfloat16)
+
+
+def dp_bit(bit):
+    return (lax.axis_index("dp") >> bit) & 1
+
+
+def dp_swap(value, bit, count):
+    return lax.ppermute(value, "dp", [(at, at ^ (1 << bit)) for at in range(count)])
+
+
+def halve(value, bit, count):
+    half = value.shape[0] // 2
+    side = dp_bit(bit)
+    keep = lax.dynamic_slice_in_dim(value, side * half, half, 0)
+    send = lax.dynamic_slice_in_dim(value, (1 - side) * half, half, 0)
+    return add_low(keep, dp_swap(send, bit, count))
+
+
+def unhalve(value, bit, count):
+    other = dp_swap(value, bit, count)
+    first = dp_bit(bit) == 0
+    return jnp.concatenate([jnp.where(first, value, other), jnp.where(first, other, value)], axis=0)
+
+
+def dp_reduce(bucket, count):
+    bits = count.bit_length() - 1
+    half = bucket.shape[0] // 2
+    done = []
+    for piece, order in ((bucket[:half], (0, 1)), (bucket[half:], (1, 0))):
+        for bit in order:
+            piece = halve(piece, bit, count)
+        for bit in range(2, bits):
+            piece = add_low(piece, dp_swap(piece, bit, count))
+        for bit in order[::-1]:
+            piece = unhalve(piece, bit, count)
+        done.append(piece)
+    return jnp.concatenate(done, axis=0)
+
+
+def columns_to_rows(value):
+    return jnp.concatenate([value[:, at : at + D] for at in range(0, value.shape[1], D)], axis=0)
+
+
+def rows_to_columns(value, rows):
+    return jnp.concatenate([value[at : at + rows] for at in range(0, value.shape[0], rows)], axis=1)
+
+
+def core_split(matrix):
+    half = matrix.shape[0] // 2
+    core = lax.axis_index("fsdp")
+    low = matrix.astype(jnp.bfloat16)
+    keep = lax.dynamic_slice_in_dim(low, core * half, half, 0)
+    send = lax.dynamic_slice_in_dim(low, (1 - core) * half, half, 0)
+    return columns_to_rows(keep), columns_to_rows(send)
 
 
 def body(
@@ -252,18 +287,19 @@
     fc2_bias,
     cotangent,
 ):
-    shards = (
-        norm_gains,
-        norm_shifts,
-        qkv_weight,
-        qv_bias,
-        rel_table,
-        proj_weight,
-        proj_bias,
-        fc1_weight,
-        fc1_bias,
-        fc2_weight,
-        fc2_bias,
+    count = lax.axis_size("dp")
+    whole = (
+        gather_cores(norm_gains, 2),
+        gather_cores(norm_shifts, 2),
+        gather_cores(qkv_weight, 1),
+        gather_cores(qv_bias, 2),
+        gather_cores(rel_table, 2),
+        gather_cores(proj_weight, 1),
+        gather_cores(proj_bias, 1),
+        gather_cores(fc1_weight, 1),
+        gather_cores(fc1_bias, 1),
+        gather_cores(fc2_weight, 1),
+        gather_cores(fc2_bias, 1),
     )
     offsets_all = jnp.arange(RELS, dtype=jnp.int32)
     onehot_full = (rel_index[:, None] == offsets_all[None, :]).astype(jnp.float32)
@@ -272,143 +308,93 @@
     region_base = jnp.where(region_win[:, :, None] == region_win[:, None, :], 0.0, -100.0).astype(
         jnp.float32
     )
-    per_batch = tokens.shape[0] // MICRO
-    region_mask = jnp.tile(region_base, (per_batch, 1, 1))
-    small_totals = [None, None]
-    factor_lists = [[], []]
-    outputs = []
-    input_grads = []
-    for batch_at in range(MICRO):
-        current = tokens[batch_at * per_batch : (batch_at + 1) * per_batch].astype(jnp.float32)
-        grad_now = cotangent[batch_at * per_batch : (batch_at + 1) * per_batch].astype(jnp.float32)
-        gathered_all = []
-        saved_all = []
-        for layer_at in range(2):
-            gathered = fetch_forward(shards, layer_at)
-            current, saved = layer_forward(
-                current, gathered, layer_at * SHIFT, region_mask if layer_at else None, onehot_low
+    region_mask = jnp.tile(region_base, (tokens.shape[0], 1, 1))
+    current = tokens.astype(jnp.float32)
+    saved_all = []
+    params_all = [tuple(item[layer_at] for item in whole) for layer_at in range(2)]
+    for layer_at in range(2):
+        current, saved = layer_forward(
+            current,
+            params_all[layer_at],
+            layer_at * SHIFT,
+            region_mask if layer_at else None,
+            onehot_low,
+        )
+        saved_all.append(saved)
+    output = current.astype(jnp.bfloat16)
+    grad_now = cotangent.astype(jnp.float32)
+    weight_sums = [None, None]
+    smalls = [None, None]
+    for layer_at in (1, 0):
+        grad_now, small, factors = layer_backward(
+            grad_now,
+            saved_all[layer_at],
+            params_all[layer_at],
+            layer_at * SHIFT,
+            region_mask if layer_at else None,
+            onehot_low,
+            onehot_full,
+        )
+        smalls[layer_at] = small
+        pairs = [
+            core_split(jnp.einsum("na,nb->ab", left, right, preferred_element_type=jnp.float32))
+            for left, right in factors
+        ]
+        buckets = []
+        for chosen in ((2, 3), (0, 1)):
+            keep = jnp.concatenate([pairs[at][0] for at in chosen], axis=0)
+            send = jnp.concatenate([pairs[at][1] for at in chosen], axis=0)
+            buckets.append(dp_reduce(add_low(keep, swap_cores(send)), count))
+        weight_sums[layer_at] = buckets
+    packed = []
+    for layer_at in range(2):
+        for item in smalls[layer_at]:
+            flat = item.reshape(-1)
+            flat = jnp.pad(flat, (0, -flat.size % D))
+            packed.append(flat.reshape(-1, D))
+    packed = jnp.concatenate(packed, axis=0)
+    rows = packed.shape[0]
+    packed = jnp.pad(packed, ((0, -rows % 128), (0, 0))).astype(jnp.bfloat16)
+    packed = dp_reduce(add_low(packed, swap_cores(packed)), count).astype(jnp.float32)
+    core = lax.axis_index("fsdp")
+    at = 0
+    small_out = [[], []]
+    for layer_at in range(2):
+        for item in smalls[layer_at]:
+            used = -(-item.size // D)
+            flat = packed[at : at + used].reshape(-1)[: item.size]
+            at += used
+            full = flat.reshape(item.shape)
+            half = item.shape[-1] // 2
+            small_out[layer_at].append(
+                lax.dynamic_slice_in_dim(full, core * half, half, full.ndim - 1)
             )
-            gathered_all.append(gathered)
-            saved_all.append(saved)
-        outputs.append(current.astype(jnp.bfloat16))
-        for layer_at in (1, 0):
-            params = fetch_backward(shards, layer_at)
-            grad_now, small, factors = layer_backward(
-                grad_now,
-                saved_all[layer_at],
-                params,
-                layer_at * SHIFT,
-                region_mask if layer_at else None,
-                onehot_low,
-                onehot_full,
-            )
-            factor_lists[layer_at].append(factors)
-            if small_totals[layer_at] is None:
-                small_totals[layer_at] = small
-            else:
-                small_totals[layer_at] = [
-                    older + newer for older, newer in zip(small_totals[layer_at], small)
-                ]
-        input_grads.append(grad_now)
-    full_grads = []
+    gains_g, shifts_g, qv_g, table_g, proj_b_g, up_b_g, down_b_g = [
+        jnp.stack([small_out[0][at], small_out[1][at]]) for at in range(7)
+    ]
+    big = [[], [], [], []]
     for layer_at in range(2):
-        matrices = []
-        for factor_at in range(4):
-            left = jnp.concatenate(
-                [entry[factor_at][0] for entry in factor_lists[layer_at]], axis=0
-            )
-            right = jnp.concatenate(
-                [entry[factor_at][1] for entry in factor_lists[layer_at]], axis=0
-            )
-            matrices.append(
-                jnp.einsum("na,nb->ab", left, right, preferred_element_type=jnp.float32)
-            )
-        small = small_totals[layer_at]
-        full_grads.append(
-            [
-                small[0],
-                small[1],
-                matrices[0],
-                small[2],
-                small[3],
-                matrices[1],
-                small[4],
-                matrices[2],
-                small[5],
-                matrices[3],
-                small[6],
-            ]
-        )
-    stacked = tuple(
-        (jnp.stack([full_grads[0][param_at], full_grads[1][param_at]]) for param_at in range(11))
-    )
-    owned = (
-        lax.psum_scatter(
-            stacked[0].astype(jnp.bfloat16), "fsdp", scatter_dimension=2, tiled=True
-        ).astype(jnp.float32),
-        lax.psum_scatter(
-            stacked[1].astype(jnp.bfloat16), "fsdp", scatter_dimension=2, tiled=True
-        ).astype(jnp.float32),
-        lax.psum_scatter(
-            stacked[2].astype(jnp.bfloat16), "fsdp", scatter_dimension=1, tiled=True
-        ).astype(jnp.float32),
-        lax.psum_scatter(
-            stacked[3].astype(jnp.bfloat16), "fsdp", scatter_dimension=2, tiled=True
-        ).astype(jnp.float32),
-        lax.psum_scatter(
-            stacked[4].astype(jnp.bfloat16), "fsdp", scatter_dimension=2, tiled=True
-        ).astype(jnp.float32),
-        lax.psum_scatter(
-            stacked[5].astype(jnp.bfloat16), "fsdp", scatter_dimension=1, tiled=True
-        ).astype(jnp.float32),
-        lax.psum_scatter(
-            stacked[6].astype(jnp.bfloat16), "fsdp", scatter_dimension=1, tiled=True
-        ).astype(jnp.float32),
-        lax.psum_scatter(
-            stacked[7].astype(jnp.bfloat16), "fsdp", scatter_dimension=1, tiled=True
-        ).astype(jnp.float32),
-        lax.psum_scatter(
-            stacked[8].astype(jnp.bfloat16), "fsdp", scatter_dimension=1, tiled=True
-        ).astype(jnp.float32),
-        lax.psum_scatter(
-            stacked[9].astype(jnp.bfloat16), "fsdp", scatter_dimension=1, tiled=True
-        ).astype(jnp.float32),
-        lax.psum_scatter(
-            stacked[10].astype(jnp.bfloat16), "fsdp", scatter_dimension=1, tiled=True
-        ).astype(jnp.float32),
-    )
-    results = lax.psum(
-        (
-            owned[0],
-            owned[1],
-            owned[2],
-            owned[3],
-            owned[4],
-            owned[5],
-            owned[6],
-            owned[7],
-            owned[8],
-            owned[9],
-            owned[10],
-        ),
-        "dp",
-    )
-    output = jnp.concatenate(outputs, axis=0)
-    tokens_grad = jnp.concatenate(input_grads, axis=0)
+        mlp, attn = weight_sums[layer_at]
+        rows = D // 2
+        big[0].append(rows_to_columns(attn[: 3 * rows], rows))
+        big[1].append(attn[3 * rows :])
+        big[2].append(rows_to_columns(mlp[: 4 * rows], rows))
+        big[3].append(mlp[4 * rows :])
+    qkv_g, proj_g, up_g, down_g = [jnp.stack(item).astype(jnp.float32) for item in big]
     return (
         output,
-        tokens_grad,
-        results[0],
-        results[1],
-        results[2],
-        results[3],
-        results[4],
-        results[5],
-        results[6],
-        results[7],
-        results[8],
-        results[9],
-        results[10],
+        grad_now,
+        gains_g,
+        shifts_g,
+        qkv_g,
+        qv_g,
+        table_g,
+        proj_g,
+        proj_b_g,
+        up_g,
+        up_b_g,
+        down_g,
+        down_b_g,
     )
 
 

time: 1050 us -> 563 us (0.54)
  blocking collectives: 557 us -> 0 us
  starting transfers between devices: 0.87 us -> 105 us
  local copies, waits for them, and re-layouts: 223 us -> 189 us
  other arithmetic: 42.7 us -> 70.1 us
  matrix products: 143 us -> 121 us
  between operations: 18.7 us -> 3.38 us
  waiting for transfers between devices: 58.1 us -> 68.8 us
    psum x1 -> x0, blocking collectives: 523 us -> none  [body(): lax.psum((owned[0], owned[1], owned[2], owned[3], owned[4], owned[5], own...]
    ppermute x0 -> x76, starting transfers between devices: none -> 105 us  [the longest x60 100 us: dp_swap(): lax.ppermute(value, 'dp', [(at, at ^ 1 << bit) for at in range(count)])]
    ppermute x0 -> x76, waiting for transfers between devices: none -> 68.8 us  [the longest x60 68.8 us: dp_swap(): lax.ppermute(value, 'dp', [(at, at ^ 1 << bit) for at in range(count)])]
    reduce_scatter x4 -> x0, waiting for transfers between devices: 56.2 us -> none  [the longest x1 16.1 us: body(): lax.psum_scatter(stacked[9].astype(jnp.bfloat16), 'fsdp', scatter_dimensi...]
    all_gather x16 -> x0, blocking collectives: 30.5 us -> none  [the longest x2 4.48 us: fetch_forward(): lax.all_gather(shards[5][layer_at], 'fsdp', axis=0, tiled=True)]
    concatenate x4 -> x12, local copies, waits for them, and re-layouts: 4.33 us -> 32.7 us  [layer_backward(): jnp.concatenate([queries_flat, keys_grad.reshape(-1, D), values_flat], ax...]
    reshape x32 -> x16, local copies, waits for them, and re-layouts: 65.2 us -> 39.1 us  [split_heads(): return rows_in.reshape(-1, WT, HEADS, HD)]
    unnamed x519 -> x281, local copies, waits for them, and re-layouts: 37.8 us -> 18.7 us
  transfers between devices with their start and end apart: 16 -> 76, of which waited for: 4 -> 40; matrix products, arithmetic and copies ran while one was open for 23% -> 25% of each run, Pallas kernels for 0% -> 0%
where the time goes in v1:
time: 563 us; the launch traced here: 557 us
  local copies, waits for them, and re-layouts  189 us (34%)
  matrix products  121 us (21%)
  starting transfers between devices  105 us (19%)
  other arithmetic  70.1 us (12%)
  waiting for transfers between devices  68.8 us (12%)
    ppermute x60, starting transfers between devices, dp_swap(): lax.ppermute(value, 'dp', [(at, at ^ 1 << bit) for at in range(count)])  100 us
    ppermute x60, waiting for transfers between devices, dp_swap(): lax.ppermute(value, 'dp', [(at, at ^ 1 << bit) for at in range(count)])  68.8 us
    reshape x16, local copies, waits for them, and re-layouts, split_heads(): return rows_in.reshape(-1, WT, HEADS, HD)  39.1 us
    concatenate x12, local copies, waits for them, and re-layouts, layer_backward(): jnp.concatenate([queries_flat, keys_grad.reshape(-1, D), values_flat], ax...  32.7 us
    dot_general x8, matrix products, body(): jnp.einsum('na,nb->ab', left, right, preferred_element_type=jnp.float32)  23.6 us
    dot_general x2, matrix products, layer_forward(): jnp.dot(normed_two, up_w, preferred_element_type=jnp.float32)  19.5 us
    unnamed x281, local copies, waits for them, and re-layouts  18.7 us
    dot_general x2, matrix products, layer_backward(): jnp.einsum('nd,fd->nf', mlp_grad, down_w, preferred_element_type=jnp.floa...  13.3 us
  transfers between devices with their start and end apart: 76, of which 40 were waited for; matrix products, arithmetic and copies ran while one was open for 25% of the time, Pallas kernels for 0%

profile of v1, /device:TPU:0, one launch (start us, length us, event | category | flops | bytes accessed | tf_op | source)
XLA Modules:
  0.0 556.8 jit_solution(5514606845417077178)
XLA Ops:
  29.3 3.4 reshape.534
  42.1 5.2 fusion.241
  68.6 9.5 %multiply_convert_fusion.3 = (bf16[392,2048]{1,0:T(8,128)(2,1)S(1)}, f32[392,2048]{1,0:T(8,128)}, f32[392,2048]{1,0:T(8,128)}) fusion(f32[2048]{0:T(1024)S(1)} %bitcast.350, bf16[392,512]{1,0:T(8,128)(2,1)S(1)} %reshape.478, bf16[2,256,2048]{2,1,0:T(8,128)(2,1)S(1)} %get-tuple-element.104, bf16[2,256,2048]{2,1,0:T(8,128)(2,1)S(1)} %get-tuple-element.105), kind=kOutput, calls=%fused_computation.45 | convolution fusion | flops 879263744 | bytes 12632064 | tf_op jit(solution)/shard_map/dot_general | solution.py:97
  108.6 5.4 fusion.242
  129.9 10.0 %multiply_convert_fusion.2 = (bf16[392,2048]{1,0:T(8,128)(2,1)}, f32[392,2048]{1,0:T(8,128)S(1)}, f32[392,2048]{1,0:T(8,128)S(1)}) fusion(f32[2048]{0:T(1024)} %bitcast.349, bf16[392,512]{1,0:T(8,128)(2,1)} %reshape.488, bf16[2,256,2048]{2,1,0:T(8,128)(2,1)} %copy-done.36, bf16[2,256,2048]{2,1,0:T(8,128)(2,1)} %copy-done.38), kind=kOutput, calls=%fused_computation.32 | convolution fusion | flops 879263744 | bytes 12632064 | tf_op jit(solution)/shard_map/dot_general | solution.py:97
  139.9 5.9 %fusion.249 = (bf16[2048]{0:T(1024)(128)(2,1)}, bf16[392,2048]{1,0:T(8,128)(2,1)}) fusion(f32[392,2048]{1,0:T(8,128)S(1)} %get-tuple-element.93, f32[392,2048]{1,0:T(8,128)S(1)} %get-tuple-element.265, bf16[392,512]{1,0:T(8,128)(2,1)S(1)} %copy-done.70, bf16[2,1024,512]{2,1,0:T(8,128)(2,1)S(1)} %copy-done.41, bf16[2,1024,512]{2,1,0:T(8,128)(2,1)S(1)} %copy-done.45), kind=kOutput, calls=%fused_computation.615 | convolution fusion | flops 838318080 | bytes 12627968 | tf_op jit(solution)/shard_map/nd,fd->nf/dot_general | solution.py:141
  148.8 4.3 convolution_convert_fusion.3
  159.8 3.8 fusion.213
  181.3 4.1 fusion.248
  189.4 4.0 multiply_reduce_fusion.1
  208.2 3.4 reshape.529
  211.6 3.6 reshape.527
  229.3 4.3 convolution_convert_fusion.4
  233.6 7.3 %fusion.246 = (bf16[2048]{0:T(1024)(128)(2,1)}, bf16[392,2048]{1,0:T(8,128)(2,1)}) fusion(f32[392,2048]{1,0:T(8,128)S(1)} %copy-done.132, f32[392,2048]{1,0:T(8,128)} %get-tuple-element.262, bf16[392,512]{1,0:T(8,128)(2,1)S(1)} %copy-done.73, bf16[2,1024,512]{2,1,0:T(8,128)(2,1)S(1)} %copy-done.47, bf16[2,1024,512]{2,1,0:T(8,128)(2,1)S(1)} %copy-done.43), kind=kOutput, calls=%fused_computation.612 | convolution fusion | flops 838318080 | bytes 12627968 | tf_op jit(solution)/shard_map/nd,fd->nf/dot_general | solution.py:141
  243.8 4.3 convolution_convert_fusion.5
  258.1 4.2 fusion.245
  265.4 3.7 multiply_reduce_fusion
  328.0 3.7 reshape.531
  440.1 3.5 collective-permute-start.47
  491.9 3.5 collective-permute-start.53
  506.4 7.1 %collective-permute-start.67 = (bf16[256,512]{1,0:T(8,128)(2,1)S(1)}, bf16[256,512]{1,0:T(8,128)(2,1)S(1)}, u32[]{:S(2)}, u32[]{:S(2)}) collective-permute-start(bf16[256,512]{1,0:T(8,128)(2,1)S(1)} %add_convert_fusion.17), channel_id=1, source_target_pairs={{0,16},{2,18},{4,20},{6,22},{8,24},{10,26},{12,28},{14,30},{16,0},... | collective-permute-start | bytes 786440 | tf_op jit(solution)/shard_map/ppermute | solution.py:224
  521.1 6.6 %collective-permute-done.67 = bf16[256,512]{1,0:T(8,128)(2,1)S(1)} collective-permute-done((bf16[256,512]{1,0:T(8,128)(2,1)S(1)}, bf16[256,512]{1,0:T(8,128)(2,1)S(1)}, u32[]{:S(2)}, u32[]{:S(2)}) %collective-permute-start.67) | collective-permute-done | bytes 262176 | tf_op jit(solution)/shard_map/ppermute | solution.py:224
  540.7 4.7 collective-permute-done.56
  546.0 5.1 collective-permute-done.63
  (788 shorter events, 432.7 us)
Async XLA Ops:
  1.4 12.9 %collective-permute-start = (bf16[2,2,256]{2,1,0:T(2,128)(2,1)}, bf16[2,2,256]{2,1,0:T(2,128)(2,1)S(1)}, u32[]{:S(2)}, u32[]{:S(2)}) collective-permute-start(bf16[2,2,256]{2,1,0:T(2,128)(2,1)} %param.18), channel_id=1, source_target_pairs={{0,1},{1,0},{2,3},{3,2},{4,5},{5,4},{6,7},{7,6},{8,9},{9,8},{10,11... | collective-permute-start | bytes 6152 | tf_op jit(solution)/shard_map/ppermute | solution.py:206
  14.2 51.6 %collective-permute-start.7 = (bf16[2,256,2048]{2,1,0:T(8,128)(2,1)}, bf16[2,256,2048]{2,1,0:T(8,128)(2,1)}, u32[]{:S(2)}, u32[]{:S(2)}) collective-permute-start(bf16[2,256,2048]{2,1,0:T(8,128)(2,1)} %param.25), channel_id=1, source_target_pairs={{0,1},{1,0},{2,3},{3,2},{4,5},{5,4},{6,7},{7,6},{8,9},{9,8},{10,11... | collective-permute-start | bytes 6291464 | tf_op jit(solution)/shard_map/ppermute | solution.py:206
  17.1 61.0 %collective-permute-start.9 = (bf16[2,1024,512]{2,1,0:T(8,128)(2,1)}, bf16[2,1024,512]{2,1,0:T(8,128)(2,1)}, u32[]{:S(2)}, u32[]{:S(2)}) collective-permute-start(bf16[2,1024,512]{2,1,0:T(8,128)(2,1)} %param.27), channel_id=1, source_target_pairs={{0,1},{1,0},{2,3},{3,2},{4,5},{5,4},{6,7},{7,6},{8,9},{9,8},{10,11... | collective-permute-start | bytes 6291464 | tf_op jit(solution)/shard_map/ppermute | solution.py:206
  311.0 104.2 %collective-permute-start.37 = (bf16[1024,512]{1,0:T(8,128)(2,1)}, bf16[1024,512]{1,0:T(8,128)(2,1)}, u32[]{:S(2)}, u32[]{:S(2)}) collective-permute-start(bf16[1024,512]{1,0:T(8,128)(2,1)} %pad_maximum_fusion.4), channel_id=1, source_target_pairs={{0,1},{1,0},{2,3},{3,2},{4,5},{5,4},{6,7},{7,6},{8,9},{9,8},{10,11... | collective-permute-start | bytes 3145736 | tf_op jit(solution)/shard_map/ppermute | solution.py:206
  338.7 14.4 %collective-permute-start.11 = (bf16[128,512]{1,0:T(8,128)(2,1)S(1)}, bf16[128,512]{1,0:T(8,128)(2,1)S(1)}, u32[]{:S(2)}, u32[]{:S(2)}) collective-permute-start(bf16[128,512]{1,0:T(8,128)(2,1)S(1)} %pad.16), channel_id=1, source_target_pairs={{0,1},{1,0},{2,3},{3,2},{4,5},{5,4},{6,7},{7,6},{8,9},{9,8},{10,11... | collective-permute-start | bytes 393224 | tf_op jit(solution)/shard_map/ppermute | solution.py:206
  340.2 80.3 %collective-permute-start.24 = (bf16[1024,512]{1,0:T(8,128)(2,1)}, bf16[1024,512]{1,0:T(8,128)(2,1)S(1)}, u32[]{:S(2)}, u32[]{:S(2)}) collective-permute-start(bf16[1024,512]{1,0:T(8,128)(2,1)} %pad_maximum_fusion.3), channel_id=1, source_target_pairs={{0,1},{1,0},{2,3},{3,2},{4,5},{5,4},{6,7},{7,6},{8,9},{9,8},{10,11... | collective-permute-start | bytes 3145736 | tf_op jit(solution)/shard_map/ppermute | solution.py:206
  350.4 116.0 %collective-permute-start.50 = (bf16[2048,512]{1,0:T(8,128)(2,1)}, bf16[2048,512]{1,0:T(8,128)(2,1)}, u32[]{:S(2)}, u32[]{:S(2)}) collective-permute-start(bf16[2048,512]{1,0:T(8,128)(2,1)} %get-tuple-element.117), channel_id=1, source_target_pairs={{0,1},{1,0},{2,3},{3,2},{4,5},{5,4},{6,7},{7,6},{8,9},{9,8},{10,11... | collective-permute-start | bytes 6291464 | tf_op jit(solution)/shard_map/ppermute | solution.py:206
  352.7 117.6 %collective-permute-start.57 = (bf16[2048,512]{1,0:T(8,128)(2,1)}, bf16[2048,512]{1,0:T(8,128)(2,1)}, u32[]{:S(2)}, u32[]{:S(2)}) collective-permute-start(bf16[2048,512]{1,0:T(8,128)(2,1)} %get-tuple-element.125), channel_id=1, source_target_pairs={{0,1},{1,0},{2,3},{3,2},{4,5},{5,4},{6,7},{7,6},{8,9},{9,8},{10,11... | collective-permute-start | bytes 6291464 | tf_op jit(solution)/shard_map/ppermute | solution.py:206
  460.4 13.7 %collective-permute-start.49 = (bf16[256,512]{1,0:T(8,128)(2,1)S(1)}, bf16[256,512]{1,0:T(8,128)(2,1)S(1)}, u32[]{:S(2)}, u32[]{:S(2)}) collective-permute-start(bf16[256,512]{1,0:T(8,128)(2,1)S(1)} %pad_maximum_fusion.21), channel_id=1, source_target_pairs={{0,4},{2,6},{4,0},{6,2},{8,12},{10,14},{12,8},{14,10},{16,20},{18,... | collective-permute-start | bytes 786440 | tf_op jit(solution)/shard_map/ppermute | solution.py:224
  461.6 13.6 %collective-permute-start.43 = (bf16[256,512]{1,0:T(8,128)(2,1)S(1)}, bf16[256,512]{1,0:T(8,128)(2,1)S(1)}, u32[]{:S(2)}, u32[]{:S(2)}) collective-permute-start(bf16[256,512]{1,0:T(8,128)(2,1)S(1)} %pad_maximum_fusion.20), channel_id=1, source_target_pairs={{0,2},{2,0},{4,6},{6,4},{8,10},{10,8},{12,14},{14,12},{16,18},{18,... | collective-permute-start | bytes 786440 | tf_op jit(solution)/shard_map/ppermute | solution.py:224
  465.3 11.6 %collective-permute-start.36 = (bf16[256,512]{1,0:T(8,128)(2,1)S(1)}, bf16[256,512]{1,0:T(8,128)(2,1)S(1)}, u32[]{:S(2)}, u32[]{:S(2)}) collective-permute-start(bf16[256,512]{1,0:T(8,128)(2,1)S(1)} %pad_maximum_fusion.19), channel_id=1, source_target_pairs={{0,4},{2,6},{4,0},{6,2},{8,12},{10,14},{12,8},{14,10},{16,20},{18,... | collective-permute-start | bytes 786440 | tf_op jit(solution)/shard_map/ppermute | solution.py:224
  466.4 11.7 %collective-permute-start.30 = (bf16[256,512]{1,0:T(8,128)(2,1)S(1)}, bf16[256,512]{1,0:T(8,128)(2,1)S(1)}, u32[]{:S(2)}, u32[]{:S(2)}) collective-permute-start(bf16[256,512]{1,0:T(8,128)(2,1)S(1)} %pad_maximum_fusion.18), channel_id=1, source_target_pairs={{0,2},{2,0},{4,6},{6,4},{8,10},{10,8},{12,14},{14,12},{16,18},{18,... | collective-permute-start | bytes 786440 | tf_op jit(solution)/shard_map/ppermute | solution.py:224
  475.2 11.6 %collective-permute-start.58 = (bf16[512,512]{1,0:T(8,128)(2,1)S(1)}, bf16[512,512]{1,0:T(8,128)(2,1)S(1)}, u32[]{:S(2)}, u32[]{:S(2)}) collective-permute-start(bf16[512,512]{1,0:T(8,128)(2,1)S(1)} %constant_dynamic-slice_fusion.38), channel_id=1, source_target_pairs={{0,2},{2,0},{4,6},{6,4},{8,10},{10,8},{12,14},{14,12},{16,18},{18,... | collective-permute-start | bytes 1572872 | tf_op jit(solution)/shard_map/ppermute | solution.py:224
  476.9 12.1 %collective-permute-start.70 = (bf16[512,512]{1,0:T(8,128)(2,1)S(1)}, bf16[512,512]{1,0:T(8,128)(2,1)S(1)}, u32[]{:S(2)}, u32[]{:S(2)}) collective-permute-start(bf16[512,512]{1,0:T(8,128)(2,1)S(1)} %constant_dynamic-slice_fusion.34), channel_id=1, source_target_pairs={{0,4},{2,6},{4,0},{6,2},{8,12},{10,14},{12,8},{14,10},{16,20},{18,... | collective-permute-start | bytes 1572872 | tf_op jit(solution)/shard_map/ppermute | solution.py:224
  483.6 11.9 %collective-permute-start.65 = (bf16[256,512]{1,0:T(8,128)(2,1)S(1)}, bf16[256,512]{1,0:T(8,128)(2,1)S(1)}, u32[]{:S(2)}, u32[]{:S(2)}) collective-permute-start(bf16[256,512]{1,0:T(8,128)(2,1)S(1)} %constant_dynamic-slice_fusion.35), channel_id=1, source_target_pairs={{0,2},{2,0},{4,6},{6,4},{8,10},{10,8},{12,14},{14,12},{16,18},{18,... | collective-permute-start | bytes 786440 | tf_op jit(solution)/shard_map/ppermute | solution.py:224
  495.7 18.3 %collective-permute-start.60 = (bf16[256,512]{1,0:T(8,128)(2,1)S(1)}, bf16[256,512]{1,0:T(8,128)(2,1)S(1)}, u32[]{:S(2)}, u32[]{:S(2)}) collective-permute-start(bf16[256,512]{1,0:T(8,128)(2,1)S(1)} %add_convert_fusion.21), channel_id=1, source_target_pairs={{0,8},{2,10},{4,12},{6,14},{8,0},{10,2},{12,4},{14,6},{16,24},{18,... | collective-permute-start | bytes 786440 | tf_op jit(solution)/shard_map/ppermute | solution.py:224
  498.3 18.9 %collective-permute-start.72 = (bf16[256,512]{1,0:T(8,128)(2,1)S(1)}, bf16[256,512]{1,0:T(8,128)(2,1)S(1)}, u32[]{:S(2)}, u32[]{:S(2)}) collective-permute-start(bf16[256,512]{1,0:T(8,128)(2,1)S(1)} %add_convert_fusion.15), channel_id=1, source_target_pairs={{0,8},{2,10},{4,12},{6,14},{8,0},{10,2},{12,4},{14,6},{16,24},{18,... | collective-permute-start | bytes 786440 | tf_op jit(solution)/shard_map/ppermute | solution.py:224
  502.3 17.2 %collective-permute-start.54 = (bf16[256,512]{1,0:T(8,128)(2,1)S(1)}, bf16[256,512]{1,0:T(8,128)(2,1)S(1)}, u32[]{:S(2)}, u32[]{:S(2)}) collective-permute-start(bf16[256,512]{1,0:T(8,128)(2,1)S(1)} %add_convert_fusion.23), channel_id=1, source_target_pairs={{0,16},{2,18},{4,20},{6,22},{8,24},{10,26},{12,28},{14,30},{16,0},... | collective-permute-start | bytes 786440 | tf_op jit(solution)/shard_map/ppermute | solution.py:224
  506.4 21.4 %collective-permute-start.67 = (bf16[256,512]{1,0:T(8,128)(2,1)S(1)}, bf16[256,512]{1,0:T(8,128)(2,1)S(1)}, u32[]{:S(2)}, u32[]{:S(2)}) collective-permute-start(bf16[256,512]{1,0:T(8,128)(2,1)S(1)} %add_convert_fusion.17), channel_id=1, source_target_pairs={{0,16},{2,18},{4,20},{6,22},{8,24},{10,26},{12,28},{14,30},{16,0},... | collective-permute-start | bytes 786440 | tf_op jit(solution)/shard_map/ppermute | solution.py:224
  514.0 16.5 %collective-permute-start.61 = (bf16[256,512]{1,0:T(8,128)(2,1)S(1)}, bf16[256,512]{1,0:T(8,128)(2,1)S(1)}, u32[]{:S(2)}, u32[]{:S(2)}) collective-permute-start(bf16[256,512]{1,0:T(8,128)(2,1)S(1)} %add_convert_fusion.20), channel_id=1, source_target_pairs={{0,16},{2,18},{4,20},{6,22},{8,24},{10,26},{12,28},{14,30},{16,0},... | collective-permute-start | bytes 786440 | tf_op jit(solution)/shard_map/ppermute | solution.py:224
  517.3 16.0 %collective-permute-start.73 = (bf16[256,512]{1,0:T(8,128)(2,1)S(1)}, bf16[256,512]{1,0:T(8,128)(2,1)S(1)}, u32[]{:S(2)}, u32[]{:S(2)}) collective-permute-start(bf16[256,512]{1,0:T(8,128)(2,1)S(1)} %add_convert_fusion.14), channel_id=1, source_target_pairs={{0,16},{2,18},{4,20},{6,22},{8,24},{10,26},{12,28},{14,30},{16,0},... | collective-permute-start | bytes 786440 | tf_op jit(solution)/shard_map/ppermute | solution.py:224
  519.5 15.0 %collective-permute-start.55 = (bf16[256,512]{1,0:T(8,128)(2,1)S(1)}, bf16[256,512]{1,0:T(8,128)(2,1)S(1)}, u32[]{:S(2)}, u32[]{:S(2)}) collective-permute-start(bf16[256,512]{1,0:T(8,128)(2,1)S(1)} %add_convert_fusion.22), channel_id=1, source_target_pairs={{0,4},{2,6},{4,0},{6,2},{8,12},{10,14},{12,8},{14,10},{16,20},{18,... | collective-permute-start | bytes 786440 | tf_op jit(solution)/shard_map/ppermute | solution.py:224
  537.1 14.0 %collective-permute-start.63 = (bf16[512,512]{1,0:T(8,128)(2,1)S(1)}, bf16[512,512]{1,0:T(8,128)(2,1)S(1)}, u32[]{:S(2)}, u32[]{:S(2)}) collective-permute-start(bf16[512,512]{1,0:T(8,128)(2,1)S(1)} %pad_maximum_fusion.11), channel_id=1, source_target_pairs={{0,2},{2,0},{4,6},{6,4},{8,10},{10,8},{12,14},{14,12},{16,18},{18,... | collective-permute-start | bytes 1572872 | tf_op jit(solution)/shard_map/ppermute | solution.py:224
  539.9 11.5 %collective-permute-start.75 = (bf16[512,512]{1,0:T(8,128)(2,1)S(1)}, bf16[512,512]{1,0:T(8,128)(2,1)S(1)}, u32[]{:S(2)}, u32[]{:S(2)}) collective-permute-start(bf16[512,512]{1,0:T(8,128)(2,1)S(1)} %pad_maximum_fusion.13), channel_id=1, source_target_pairs={{0,4},{2,6},{4,0},{6,2},{8,12},{10,14},{12,8},{14,10},{16,20},{18,... | collective-permute-start | bytes 1572872 | tf_op jit(solution)/shard_map/ppermute | solution.py:224
  (185 other events, 1145.4 us)
